TPU v7x, 512 devices: a whole 4x4x16 slice. The times are simulated.
512 devices in a mesh: ctx: 32 (over z, core), head: 8 (over y, x_lo), dp: 2 (over x_hi).
Axes of the slice: x: 4 (x_hi: 2, x_lo: 2; x = x_hi * 2 + x_lo), y: 4, z: 16, core: 2. Of those that a mesh axis runs over, the one named last changes fastest.
Arguments:
- queries: bfloat16 [16384, 4096], P(('dp', 'ctx'), 'head'), parts along dimension 0, may hold values from -12 to 12
- keys_values: bfloat16 [2, 16384, 1024], P(None, ('dp', 'ctx'), 'head'), parts along dimension 1, may hold values from -12 to 12
- positions: int32 [16384], P(('dp', 'ctx')), parts along dimension 0, may hold values from 0 to 4096, as said below
- offsets: int32 [16], P('dp'), parts along dimension 0, may hold values from 0 to 8190, as said below
- w_out: bfloat16 [4096, 4096], P('head'), may hold values from -0.375 to 0.375
Outputs:
- mixed: bfloat16 [16384, 4096], P(('dp', 'ctx'), 'head'), parts along dimension 0
There are 2 independent parts, one for each index of `dp`. A program takes and returns all parts, laid end to end along the dimension named above; an argument that names none is the same for every part. Nothing has to cross between parts.
Inputs may be any that keep to these rules, and one draw needn't show every extreme that they name: offsets[0] = 0 and the offsets rise strictly; the first document holds exactly 4097 tokens and every later one two or more. positions[t] = t minus the largest offset not above t.
All inputs are finite; a program needn't handle non-finite values.
Results may differ from a plain program's by a relative error of at most 0.02.
Values may be sent and summed in bfloat16 or wider, within the bound.
A program may use at most 128 MiB of HBM per device.

v0:
```python
import math

import jax
import jax.numpy as jnp
from jax import lax
from jax.sharding import PartitionSpec as P

HD = 128


ROPE_BASE = 500000.0
STRETCH = 16.0
ANCHOR_LENGTH = 8192.0
BETA_FAST = 32.0
BETA_SLOW = 1.0
MAGNITUDE = 0.1 * math.log(16.0) + 1.0
NEGATIVE = -1e30


def tables(positions, width):
    half = width // 2
    index = jnp.arange(half, dtype=jnp.float32)
    base_freq = jnp.exp(index * (-2.0 * math.log(ROPE_BASE) / width))
    ratio = base_freq * (ANCHOR_LENGTH / (2.0 * math.pi))
    ramp = jnp.clip((ratio - BETA_SLOW) / (BETA_FAST - BETA_SLOW), 0.0, 1.0)
    freq = base_freq * (1.0 - ramp) / STRETCH + base_freq * ramp
    angle = positions.astype(jnp.float32)[:, None] * freq[None, :]
    return (jnp.cos(angle) * MAGNITUDE, jnp.sin(angle) * MAGNITUDE)


def rotate(field, cosine, sine):
    half = field.shape[-1] // 2
    first = field[..., :half]
    second = field[..., half:]
    cos_rows = cosine[:, None, :]
    sin_rows = sine[:, None, :]
    return jnp.concatenate(
        [first * cos_rows - second * sin_rows, second * cos_rows + first * sin_rows], axis=-1
    )


def shards(queries, keys_values, positions, offsets, w_out):
    rows = queries.shape[0]
    heads_here = w_out.shape[0] // HD
    cosine, sine = tables(positions, HD)
    rot_queries = (
        rotate(queries.reshape(rows, heads_here, HD).astype(jnp.float32), cosine, sine)
        * HD ** (-0.5)
    ).astype(jnp.bfloat16)
    rot_keys = (
        rotate(keys_values[0].reshape(rows, 1, HD).astype(jnp.float32), cosine, sine)
        .reshape(rows, HD)
        .astype(jnp.bfloat16)
    )
    moving = jnp.stack([rot_keys, keys_values[1]])
    first = lax.axis_index("ctx") * rows
    query_index = first + jnp.arange(rows, dtype=jnp.int32)
    starts = jnp.max(
        jnp.where(offsets[None, :] <= query_index[:, None], offsets[None, :], 0), axis=1
    )
    piece = lax.all_gather(moving, "ctx", axis=1, tiled=True)
    key_rows = piece[0]
    value_rows = piece[1]
    count = key_rows.shape[0]
    key_index = jnp.arange(count, dtype=jnp.int32)
    visible = (
        (key_index[None, :] <= query_index[:, None]) & (key_index[None, :] >= starts[:, None])
    )[:, None, :]
    scores = jnp.einsum("qhd,kd->qhk", rot_queries, key_rows, preferred_element_type=jnp.float32)
    peak = jnp.full((rows, heads_here), NEGATIVE, jnp.float32)
    new_peak = jnp.maximum(peak, jnp.max(jnp.where(visible, scores, NEGATIVE), axis=2))
    expo = jnp.where(visible, jnp.exp(scores - new_peak[..., None]), 0.0)
    total = jnp.sum(expo, axis=2)
    accum = jnp.einsum(
        "qhk,kd->qhd", expo.astype(jnp.bfloat16), value_rows, preferred_element_type=jnp.float32
    )
    result = (new_peak, total, accum)
    peak, total, accum = result
    attended = (accum / total[..., None]).astype(jnp.bfloat16).reshape(rows, heads_here * HD)
    partial_value = jnp.dot(attended, w_out, preferred_element_type=jnp.float32)
    return lax.psum_scatter(
        partial_value.astype(jnp.bfloat16), "head", scatter_dimension=1, tiled=True
    )


def solution(mesh):
    in_specs = (
        P(("dp", "ctx"), "head"),
        P(None, ("dp", "ctx"), "head"),
        P(("dp", "ctx")),
        P("dp"),
        P("head", None),
    )
    out_specs = P(("dp", "ctx"), "head")
    return jax.shard_map(shards, mesh=mesh, in_specs=in_specs, out_specs=out_specs, check_vma=False)
```

profile of v0, /device:TPU:1, one launch (start us, length us, event | category | flops | bytes accessed | tf_op | source)
XLA Modules:
  0.0 207.3 jit_solution(4234741551339588215)
XLA Ops:
  6.5 0.0 all-gather.2.cloned.1.call-start
  6.6 0.7 convert_element_type.48
  7.2 0.9 fusion.32
  8.1 0.1 copy.25
  8.3 0.1 copy.26
  8.4 0.3 fusion.22
  8.7 0.7 pad_maximum_fusion
  9.4 0.0 all-gather.2.cloned.1.call-update
  9.4 0.0 reduce-scatter.2.cloned.1.call-start
  9.5 1.1 copy.15
  10.6 0.2 copy.24
  10.8 0.2 copy.23
  11.0 0.7 select_reduce_fusion.1
  11.8 0.5 fusion.16
  12.3 0.1 multiply_subtract_fusion
  12.4 2.0 fusion.5
  14.4 80.9 %all-gather.2.cloned.1.call-done = bf16[2,8192,128]{1,2,0:T(8,128)(2,1)} async-done(((bf16[2,256,128]{1,2,0:T(8,128)(2,1)}), bf16[2,8192,128]{1,2,0:T(8,128)(2,1)}) %all-gather.2.cloned.1.call-update) | async-done | bytes 4194320 | tf_op jit(solution)/shard_map/all_gather | solution.py:61
  95.4 15.2 %select_reduce_fusion = (f32[256,4]{0,1:T(4,128)S(1)}, f32[256,4,8192]{2,0,1:T(8,128)}) fusion(pred[256,8192]{1,0:T(8,128)(4,1)S(1)} %fusion.5, bf16[2,8192,128]{1,2,0:T(8,128)(2,1)} %all-gather.2.cloned.1.call-done, f32[256,4,64]{2,0,1:T(8,128)S(1)} %get-tuple-element.6, f32[256,4,64]{2,0,1:T(8,128)S(1)} %get-tuple-element.5), kind=kOutput, calls=%fused_computation.1 | convolution fusion | flops 2164653056 | bytes 38277120 | tf_op jit(solution)/shard_map/qhd,kd->qhk/dot_general | solution.py:69
  110.5 14.7 %fusion = f32[256,4]{0,1:T(4,128)S(1)} fusion(f32[256,4,8192]{2,0,1:T(8,128)} %get-tuple-element.16, f32[256,4]{0,1:T(4,128)S(1)} %broadcast_maximum_fusion, pred[256,8192]{1,0:T(8,128)(4,1)S(1)} %fusion.5), kind=kLoop, calls=%fused_computation.2 | loop fusion | flops 25164800 | bytes 35659776 | tf_op jit(solution)/shard_map/reduce_sum | solution.py:73
  125.2 14.3 %fusion.10 = bf16[256,4,128]{0,2,1:T(8,128)(2,1)S(1)} fusion(bf16[2,8192,128]{1,2,0:T(8,128)(2,1)} %all-gather.2.cloned.1.call-done, f32[256,4,8192]{2,0,1:T(8,128)} %get-tuple-element.16, f32[256,4]{0,1:T(4,128)S(1)} %broadcast_maximum_fusion, pred[256,8192]{1,0:T(8,128)(4,1)S(1)} %fusion.5, f32[256,4]{0,1:T(4,128)S(1)} %fusion), kind=kOutput, calls=%fused_computation.14 | convolution fusion | flops 2172911616 | bytes 38019072 | tf_op jit(solution)/shard_map/qhk,kd->qhd/dot_general | solution.py:74
  139.5 4.8 %convolution_convert_fusion = bf16[256,4096]{1,0:T(8,128)(2,1)} fusion(bf16[256,512]{0,1:T(8,128)(2,1)S(1)} %bitcast.26, bf16[512,4096]{1,0:T(8,128)(2,1)} %param.9), kind=kOutput, calls=%fused_computation.9 | convolution fusion | flops 1074790400 | bytes 6553600 | tf_op jit(solution)/shard_map/dot_general | solution.py:80
  144.3 0.0 reduce-scatter.2.cloned.1.call-update
  144.3 56.2 %reduce-scatter.2.cloned.1.call-done = bf16[256,512]{1,0:T(8,128)(2,1)} async-done(((bf16[256,4096]{1,0:T(8,128)(2,1)}), bf16[256,512]{1,0:T(8,128)(2,1)}) %reduce-scatter.2.cloned.1.call-update) | async-done | bytes 262160 | tf_op jit(solution)/shard_map/reduce_scatter | solution.py:81
  (6 shorter events, 0.1 us)
Async XLA Ops:
  6.5 88.8 %all-gather.2.cloned.1.call-start = ((), (), s32[]{:S(2)}) async-start(), calls=%async_computation.1 | async-start | bytes 4325376 | tf_op jit(solution)/shard_map/all_gather | solution.py:61
  9.4 191.1 %reduce-scatter.2.cloned.1.call-start = ((), (), s32[]{:S(2)}) async-start(), calls=%async_computation.2 | async-start | bytes 2359296 | tf_op jit(solution)/shard_map/reduce_scatter | solution.py:81
Sparse Core Ops, SparseCore 0:
  9.5 85.7 all-gather.1
  144.4 56.0 reduce-scatter.1
where the time goes:
time: 208 us; the launch traced here: 207 us
  waiting for transfers between devices  137 us (66%)
  matrix products  34.2 us (16%)
  other arithmetic  19.8 us (10%)
  between operations  13.5 us (6%)
  local copies, waits for them, and re-layouts  2.61 us (1%)
    all_gather x1, waiting for transfers between devices, shards(): piece = lax.all_gather(moving, 'ctx', axis=1, tiled=True)  80.9 us
    reduce_scatter x1, waiting for transfers between devices, shards(): lax.psum_scatter(partial_value.astype(jnp.bfloat16), 'head', scatter_dime...  56.2 us
    dot_general x1, matrix products, shards(): jnp.einsum('qhd,kd->qhk', rot_queries, key_rows, preferred_element_type=j...  15.2 us
    reduce_sum x1, other arithmetic, shards(): total = jnp.sum(expo, axis=2)  14.7 us
    dot_general x1, matrix products, shards(): jnp.einsum('qhk,kd->qhd', expo.astype(jnp.bfloat16), value_rows, preferre...  14.3 us
    dot_general x1, matrix products, shards(): partial_value = jnp.dot(attended, w_out, preferred_element_type=jnp.float32)  4.81 us
  transfers between devices with their start and end apart: 2, of which 2 were waited for; matrix products, arithmetic and copies ran while one was open for 2% of the time, Pallas kernels for 0%

commit v1 on v0

v1 whole, which is shorter than its diff:
```python
import functools
import math

import jax
import jax.numpy as jnp
from jax import lax
from jax.experimental import pallas as pl
from jax.experimental.pallas import tpu as pltpu
from jax.sharding import PartitionSpec as P

HD = 128
QH = 4
ROPE_BASE = 500000.0
STRETCH = 16.0
ANCHOR_LENGTH = 8192.0
BETA_FAST = 32.0
BETA_SLOW = 1.0
MAGNITUDE = 0.1 * math.log(16.0) + 1.0
NEGATIVE = -1e30
LOG2E = 1.4426950408889634
MESH = pl.DeviceIdType.MESH
BF = jnp.bfloat16
F32 = jnp.float32


def remote(src, dst, send_sem, recv_sem, device):
    return pltpu.make_async_remote_copy(
        src_ref=src, dst_ref=dst, send_sem=send_sem, recv_sem=recv_sem,
        device_id=device, device_id_type=MESH,
    )


def dot(a, b):
    return jnp.dot(a, b, preferred_element_type=F32)


def dot_t(a, b):
    return lax.dot_general(a, b, (((1,), (1,)), ((), ())), preferred_element_type=F32)


def kernel(
    nc, nh, rows,
    q_ref, kv_ref, off_ref, w_ref, out_ref,
    qs, kvb, st, mx, acc, w2, att, attp, ysb, yrb, xq, xp, xr,
    up_s, peer_s, kv_r, wl_s, ws_s, wr_s, wf_s, wf_r, ax_s, ax_r, y_s, y_r, xq_s, xq_r, xr_s, xr_r,
):
    nhalf = nc // 2
    nz = nhalf // 2
    ny = nh // 2
    half_rows = rows // 2
    mrows = 2 * half_rows
    width = QH * HD
    wrows = width // 2

    c = lax.axis_index("ctx")
    hd = lax.axis_index("head")
    dp = lax.axis_index("dp")
    z = c // 2
    core = c % 2
    half = z // nz
    zz = z % nz
    own = 2 * zz + core
    other = 2 * zz + 1 - core
    y = hd // 2
    x = hd % 2
    up = {"ctx": jnp.minimum(c + 2, nc - 1)}
    down = {"ctx": jnp.maximum(c - 2, 0)}
    peer = {"ctx": c + 1 - 2 * core}
    across = {"head": hd + 1 - 2 * x}
    same_dp = x == core
    w_to = {"head": hd + 1 - 2 * x, "dp": jnp.where(same_dp, dp, 1 - dp)}
    w_from = {"head": hd + 1 - 2 * x, "dp": jnp.where(same_dp, 1 - dp, dp)}
    extra = nhalf

    def along_y(j):
        return {"head": ((y + j) % ny) * 2 + x}

    barrier = pltpu.get_barrier_semaphore()

    def greet(device):
        pl.semaphore_signal(barrier, inc=1, device_id=device, device_id_type=MESH)

    greet(peer)
    greet(across)
    greet(w_to)
    greet(w_from)
    for j in range(1, ny):
        greet(along_y(j))

    @pl.when(zz < nz - 1)
    def _():
        greet(up)

    @pl.when(zz > 0)
    def _():
        greet(down)

    @pl.when(c < nhalf)
    def _():
        greet({"ctx": jnp.int32(extra)})

    @pl.when(c == extra)
    def _():
        def body(d, carry):
            greet({"ctx": d})
            return carry
        lax.fori_loop(0, nhalf, body, 0)

    def own_weights(j):
        col = pl.multiple_of((((y + j) % ny) * 2 + x) * width, 128)
        return pltpu.make_async_copy(
            w_ref.at[:, pl.ds(col, width)], w2.at[j, pl.ds(0, width), :], wl_s.at[j])

    for j in range(ny):
        own_weights(j).start()

    lane = lax.broadcasted_iota(jnp.int32, (rows, HD), 1)
    token = lax.broadcasted_iota(jnp.int32, (rows, HD), 0) + c * rows
    start = jnp.zeros((rows, HD), jnp.int32)
    for d in range(off_ref.shape[0]):
        o = off_ref[d]
        start = jnp.maximum(start, jnp.where(token >= o, o, 0))
    st[...] = start
    index = (lax.broadcasted_iota(jnp.int32, (8, HD), 1) % (HD // 2)).astype(F32)
    base = jnp.exp(index * (-2.0 * math.log(ROPE_BASE) / HD))
    ramp = jnp.clip((base * (ANCHOR_LENGTH / (2.0 * math.pi)) - BETA_SLOW) / (BETA_FAST - BETA_SLOW), 0.0, 1.0)
    freq = base * (1.0 - ramp) / STRETCH + base * ramp
    angle = (token - start).astype(F32) * freq[0:1]
    cosine = jnp.cos(angle) * MAGNITUDE
    sine = jnp.sin(angle) * jnp.where(lane < HD // 2, -MAGNITUDE, MAGNITUDE)

    def rotate(field):
        field = field.astype(F32)
        return field * cosine + pltpu.roll(field, HD // 2, 1) * sine

    kvb[own, 1] = kv_ref[1]
    kvb[own, 0] = rotate(kv_ref[0]).astype(BF)

    pl.semaphore_wait(
        barrier,
        4 + (ny - 1)
        + jnp.where(zz < nz - 1, 1, 0) + jnp.where(zz > 0, 1, 0)
        + jnp.where(c < nhalf, 1, 0) + jnp.where(c == extra, nhalf, 0),
    )

    def send_up(slot, i, step):
        return remote(kvb.at[slot, i], kvb.at[slot, i], up_s.at[step, i], kv_r.at[slot, i], up)

    def send_peer(slot, i, step):
        return remote(kvb.at[slot, i], kvb.at[slot, i], peer_s.at[step, i], kv_r.at[slot, i], peer)

    @pl.when(zz < nz - 1)
    def _():
        for i in (1, 0):
            send_up(own, i, 0).start()
    for i in (1, 0):
        send_peer(own, i, 0).start()

    wrow = pl.multiple_of(core * wrows, 128)
    wback = pl.multiple_of((1 - core) * wrows, 128)

    def send_weights(j):
        col = pl.multiple_of((((y + j) % ny) * 2 + 1 - x) * width, 128)
        return remote(
            w_ref.at[pl.ds(wrow, wrows), pl.ds(col, width)],
            w2.at[j, pl.ds(width + wrow, wrows), :], ws_s.at[j], wr_s.at[j], w_to)

    def pass_weights(j):
        at = w2.at[j, pl.ds(width + wrow, wrows), :]
        return remote(at, at, wf_s.at[j], wf_r.at[j], peer)

    def passed_weights(j):
        at = w2.at[j, pl.ds(width + wback, wrows), :]
        return remote(at, at, wf_s.at[j], wf_r.at[j], peer)

    for j in range(ny):
        send_weights(j).start()

    def forward_weights():
        for j in range(ny):
            send_weights(j).wait_recv()
            pass_weights(j).start()

    scale = HD ** (-0.5) * LOG2E
    for h in range(QH):
        rot = (rotate(q_ref[:, h * HD:(h + 1) * HD]) * scale).astype(BF)
        for r in range(2):
            at = (r * QH + h) * half_rows
            qs[at:at + half_rows, :] = rot[r * half_rows:(r + 1) * half_rows]

    def send_xq(d):
        return remote(xq, xq, xq_s.at[d], xq_r, {"ctx": d})

    @pl.when(c == extra)
    def _():
        heads = [qs[h * half_rows:h * half_rows + 1, :] for h in range(QH)]
        xq[...] = jnp.concatenate(heads + [jnp.zeros((16 - QH, HD), BF)], axis=0)

        def body(d, carry):
            send_xq(d).start()
            return carry
        lax.fori_loop(0, nhalf, body, 0)

    def with_ones(v):
        return jnp.concatenate([v, jnp.ones(v.shape, BF)], axis=1)

    def wide(v, n):
        return jnp.tile(v, (1, n))

    def starts_of(t):
        r = t // (QH // 2)
        part = st[r * half_rows:(r + 1) * half_rows, :]
        return jnp.concatenate([part] * 2, axis=0)

    def tokens_of(t, n):
        r = t // (QH // 2)
        i = lax.broadcasted_iota(jnp.int32, (mrows, n), 0) % half_rows
        return i + (c * rows + r * half_rows)

    ntile = QH

    for t in range(ntile):
        at = slice(t * mrows, (t + 1) * mrows)
        s = dot_t(qs[at, :], kvb[own, 0])
        key = lax.broadcasted_iota(jnp.int32, (mrows, rows), 1) + c * rows
        seen = (key <= tokens_of(t, rows)) & (key >= wide(starts_of(t), rows // HD))
        s = jnp.where(seen, s, NEGATIVE)
        m = jnp.broadcast_to(jnp.max(s, axis=1, keepdims=True), (mrows, HD))
        p = jnp.exp2(s - wide(m, rows // HD)).astype(BF)
        mx[at, :] = m
        acc[at, :] = dot(p, with_ones(kvb[own, 1]))

    def update(first, keys, values, masked):
        n = keys.shape[0]
        values = with_ones(values)
        for t in range(ntile):
            at = slice(t * mrows, (t + 1) * mrows)
            s = dot_t(qs[at, :], keys)
            if masked:
                key = lax.broadcasted_iota(jnp.int32, (mrows, n), 1) + first
                s = jnp.where(key >= wide(starts_of(t), n // HD), s, NEGATIVE)
            before = mx[at, :]
            m = jnp.maximum(before, jnp.max(s, axis=1, keepdims=True))
            p = jnp.exp2(s - wide(m, n // HD)).astype(BF)
            alpha = jnp.exp2(before - m)
            mx[at, :] = m
            acc[at, :] = acc[at, :] * wide(alpha, 2) + dot(p, values)

    def send_xp():
        return remote(xp, xr.at[own], xr_s, xr_r.at[own], {"ctx": jnp.int32(extra)})

    @pl.when(c < nhalf)
    def _():
        send_xq(0).wait_recv()
        s = dot_t(xq[...], kvb[own, 0])
        m = jnp.broadcast_to(jnp.max(s, axis=1, keepdims=True), (16, HD))
        p = jnp.exp2(s - wide(m, rows // HD)).astype(BF)
        xp[:, 0:HD] = m[0:8]
        xp[:, HD:] = dot(p, with_ones(kvb[own, 1]))[0:8]
        send_xp().start()

    for i in (1, 0):
        send_peer(other, i, 0).wait_recv()

    @pl.when(core == 1)
    def _():
        update((c - 1) * rows, kvb[other, 0], kvb[other, 1], True)

    late = min(5, nz - 1)

    def step(k, carry):
        chip = zz - k
        mine = 2 * chip + core
        theirs = 2 * chip + 1 - core
        for i in (1, 0):
            send_up(mine, i, 0).wait_recv()

            @pl.when(zz < nz - 1)
            def _():
                send_up(mine, i, k).start()
            send_peer(mine, i, k).start()
        for i in (1, 0):
            send_peer(theirs, i, 0).wait_recv()
        keys = jnp.concatenate([kvb[2 * chip, 0], kvb[2 * chip + 1, 0]], axis=0)
        values = jnp.concatenate([kvb[2 * chip, 1], kvb[2 * chip + 1, 1]], axis=0)

        @pl.when(half == 0)
        def _():
            update(0, keys, values, False)

        @pl.when(half == 1)
        def _():
            update((half * nhalf + 2 * chip) * rows, keys, values, True)

        @pl.when(k == late)
        def _():
            forward_weights()
        return carry

    lax.fori_loop(1, zz + 1, step, 0)

    @pl.when(zz < late)
    def _():
        forward_weights()

    @pl.when(c == extra)
    def _():
        def arrived(d, carry):
            remote(xp, xr.at[d], xr_s, xr_r.at[d], {"ctx": jnp.int32(0)}).wait_recv()
            return carry
        lax.fori_loop(0, nhalf, arrived, 0)
        pad = [jnp.zeros((8 - QH, HD), F32)]
        mo = jnp.concatenate([mx[h * half_rows:h * half_rows + 1, :] for h in range(QH)] + pad, axis=0)
        ao = jnp.concatenate(
            [acc[h * half_rows:h * half_rows + 1, :] for h in range(QH)]
            + [jnp.zeros((8 - QH, 2 * HD), F32)], axis=0)
        m = mo
        for d in range(nhalf):
            m = jnp.maximum(m, xr[d, :, 0:HD])
        total = ao * wide(jnp.exp2(mo - m), 2)
        for d in range(nhalf):
            total = total + xr[d, :, HD:] * wide(jnp.exp2(xr[d, :, 0:HD] - m), 2)
        for h in range(QH):
            acc[h * half_rows:h * half_rows + 1, :] = total[h:h + 1, :]

    def send_att(r):
        return remote(att.at[r], attp.at[r], ax_s.at[r], ax_r.at[r], across)

    for r in range(2):
        for h in range(QH):
            at = (r * QH + h) * half_rows
            block = acc[at:at + half_rows, :]
            att[r, :, h * HD:(h + 1) * HD] = (block[:, 0:HD] / block[:, HD:]).astype(BF)
        send_att(r).start()

    for j in range(ny):
        own_weights(j).wait()
        passed_weights(j).wait_recv()

    def send_y(r, j):
        return remote(ysb.at[r, j], yrb.at[r, j], y_s.at[r, j], y_r.at[r, j], along_y(j))

    order = sorted(range(1, ny), key=lambda j: -min(j, ny - j))
    for r in range(2):
        send_att(r).wait_recv()
        for j in order + [0]:
            part = dot(att[r], w2[j, 0:width, :]) + dot(attp[r], w2[j, width:, :])
            ysb[r, j] = part.astype(BF)
            if j:
                send_y(r, j).start()

    for r in range(2):
        total = ysb[r, 0].astype(F32)
        for j in order[::-1]:
            send_y(r, j).wait_recv()
            total = total + yrb[r, j].astype(F32)
        out_ref[r * half_rows:(r + 1) * half_rows, :] = total.astype(BF)

    for r in range(2):
        send_att(r).wait_send()
        for j in order:
            send_y(r, j).wait_send()
    for j in range(ny):
        send_weights(j).wait_send()
        pass_weights(j).wait_send()

    def sent(k, carry):
        for i in (1, 0):
            @pl.when(zz < nz - 1)
            def _():
                send_up(own, i, k).wait_send()
            send_peer(own, i, k).wait_send()
        return carry
    lax.fori_loop(0, zz + 1, sent, 0)

    @pl.when(c < nhalf)
    def _():
        send_xp().wait_send()

    @pl.when(c == extra)
    def _():
        def body(d, carry):
            send_xq(d).wait_send()
            return carry
        lax.fori_loop(0, nhalf, body, 0)


def shards(nc, nh, queries, keys_values, offsets, w_out):
    rows = queries.shape[0]
    width = QH * HD
    nhalf = nc // 2
    nz = nhalf // 2
    ny = nh // 2
    half_rows = rows // 2
    dma = pltpu.SemaphoreType.DMA
    vmem = pl.BlockSpec(memory_space=pltpu.VMEM)
    return pl.pallas_call(
        functools.partial(kernel, nc, nh, rows),
        out_shape=jax.ShapeDtypeStruct((rows, width), BF),
        in_specs=[vmem, vmem, pl.BlockSpec(memory_space=pltpu.SMEM), pl.BlockSpec(memory_space=pl.ANY)],
        out_specs=vmem,
        scratch_shapes=[
            pltpu.VMEM((QH * rows, HD), BF),
            pltpu.VMEM((nhalf, 2, rows, HD), BF),
            pltpu.VMEM((rows, HD), jnp.int32),
            pltpu.VMEM((QH * rows, HD), F32),
            pltpu.VMEM((QH * rows, 2 * HD), F32),
            pltpu.VMEM((ny, 2 * width, width), BF),
            pltpu.VMEM((2, half_rows, width), BF),
            pltpu.VMEM((2, half_rows, width), BF),
            pltpu.VMEM((2, ny, half_rows, width), BF),
            pltpu.VMEM((2, ny, half_rows, width), BF),
            pltpu.VMEM((16, HD), BF),
            pltpu.VMEM((8, 3 * HD), F32),
            pltpu.VMEM((nhalf, 8, 3 * HD), F32),
            dma((nz, 2)), dma((nz, 2)), dma((nhalf, 2)),
            dma((ny,)), dma((ny,)), dma((ny,)), dma((ny,)), dma((ny,)),
            dma((2,)), dma((2,)),
            dma((2, ny)), dma((2, ny)),
            dma((nhalf,)), dma, dma, dma((nhalf,)),
        ],
        compiler_params=pltpu.CompilerParams(
            collective_id=0, has_side_effects=True, vmem_limit_bytes=40 * 1024 * 1024),
        cost_estimate=pl.CostEstimate(flops=4 * 10 ** 9, bytes_accessed=6 * 2 ** 20, transcendentals=4 * 2 ** 20),
    )(queries, keys_values, offsets, w_out)


def solution(mesh):
    nc, nh = mesh.shape["ctx"], mesh.shape["head"]

    def program(queries, keys_values, positions, offsets, w_out):
        return shards(nc, nh, queries, keys_values, offsets, w_out)

    in_specs = (
        P(("dp", "ctx"), "head"),
        P(None, ("dp", "ctx"), "head"),
        P(("dp", "ctx")),
        P("dp"),
        P("head", None),
    )
    out_specs = P(("dp", "ctx"), "head")
    return jax.shard_map(program, mesh=mesh, in_specs=in_specs, out_specs=out_specs, check_vma=False)
```

time: 208 us -> 65.2 us (0.31)
  the two profiles are of different devices: /device:TPU:1 before, /device:TPU:227 now
where the time goes in v1:
time: 65.2 us; the launch traced here: 65 us
  Pallas kernels  59.6 us (91%)
  local copies, waits for them, and re-layouts  5.4 us (8%)
    pallas_call x1, Pallas kernels, shards(): pl.pallas_call(functools.partial(kernel, nc, nh, rows), out_shape=jax.Sha...  59.6 us
    unnamed x9, local copies, waits for them, and re-layouts  5.4 us

profile of v1, /device:TPU:227, one launch (start us, length us, event | category | flops | bytes accessed | tf_op | source)
XLA Modules:
  0.0 65.0 jit_solution(4974514028784664777)
XLA Ops:
  0.0 0.0 copy-start
  0.0 2.2 %copy-done = bf16[512,4096]{1,0:T(8,128)(2,1)S(1)} copy-done((bf16[512,4096]{1,0:T(8,128)(2,1)S(1)}, bf16[512,4096]{1,0:T(8,128)(2,1)}, u32[]{:S(2)}) %copy-start) | copy-done | bytes 4194328
  2.2 0.0 copy-start.1
  2.2 0.9 %copy-done.1 = bf16[256,512]{1,0:T(8,128)(2,1)S(1)} copy-done((bf16[256,512]{1,0:T(8,128)(2,1)S(1)}, bf16[256,512]{1,0:T(8,128)(2,1)}, u32[]{:S(2)}) %copy-start.1) | copy-done | bytes 262168
  3.1 0.0 copy-start.2
  3.1 0.9 %copy-done.2 = bf16[2,256,128]{2,1,0:T(8,128)(2,1)S(1)} copy-done((bf16[2,256,128]{2,1,0:T(8,128)(2,1)S(1)}, bf16[2,256,128]{2,1,0:T(8,128)(2,1)}, u32[]{:S(2)}) %copy-start.2) | copy-done | bytes 131096
  4.0 0.0 copy-start.3
  4.0 0.7 %copy-done.3 = s32[8]{0:T(128)S(1)} copy-done((s32[8]{0:T(128)S(1)}, s32[8]{0:T(128)}, u32[]{:S(2)}) %copy-start.3) | copy-done | bytes 56
  4.7 59.6 %shard_map.46 = bf16[256,512]{1,0:T(8,128)(2,1)S(1)} custom-call(bf16[256,512]{1,0:T(8,128)(2,1)S(1)} %copy-done.1, bf16[2,256,128]{2,1,0:T(8,128)(2,1)S(1)} %copy-done.2, s32[8]{0:T(128)S(1)} %copy-done.3, bf16[512,4096]{1,0:T(8,128)(2,1)S(1)} %copy-done), custom_call_target="tpu_custom_call" | custom-call | flops 4000000000 | bytes 6291456 | tf_op jit(solution)/shard_map/pallas_call | solution.py:397
  64.3 0.7 %copy.6 = bf16[256,512]{1,0:T(8,128)(2,1)} copy(bf16[256,512]{1,0:T(8,128)(2,1)S(1)} %shard_map.46) | data formatting | bytes 524288
Async XLA Ops:
  0.0 2.2 %copy-start = (bf16[512,4096]{1,0:T(8,128)(2,1)S(1)}, bf16[512,4096]{1,0:T(8,128)(2,1)}, u32[]{:S(2)}) copy-start(bf16[512,4096]{1,0:T(8,128)(2,1)} %w_ref.1) | copy-start | bytes 12582916
  2.2 0.9 %copy-start.1 = (bf16[256,512]{1,0:T(8,128)(2,1)S(1)}, bf16[256,512]{1,0:T(8,128)(2,1)}, u32[]{:S(2)}) copy-start(bf16[256,512]{1,0:T(8,128)(2,1)} %q_ref.1) | copy-start | bytes 786436
  3.1 0.9 %copy-start.2 = (bf16[2,256,128]{2,1,0:T(8,128)(2,1)S(1)}, bf16[2,256,128]{2,1,0:T(8,128)(2,1)}, u32[]{:S(2)}) copy-start(bf16[2,256,128]{2,1,0:T(8,128)(2,1)} %kv_ref.1) | copy-start | bytes 393220
  4.0 0.7 %copy-start.3 = (s32[8]{0:T(128)S(1)}, s32[8]{0:T(128)}, u32[]{:S(2)}) copy-start(s32[8]{0:T(128)} %off_ref.1) | copy-start | bytes 100

commit v2 on v1

--- a/solution.py
+++ b/solution.py
@@ -10,6 +10,7 @@
 
 HD = 128
 QH = 4
+NR = 4
 ROPE_BASE = 500000.0
 STRETCH = 16.0
 ANCHOR_LENGTH = 8192.0
@@ -40,17 +41,19 @@
 
 def kernel(
     nc, nh, rows,
-    q_ref, kv_ref, off_ref, w_ref, out_ref,
-    qs, kvb, st, mx, acc, w2, att, attp, ysb, yrb, xq, xp, xr,
-    up_s, peer_s, kv_r, wl_s, ws_s, wr_s, wf_s, wf_r, ax_s, ax_r, y_s, y_r, xq_s, xq_r, xr_s, xr_r,
+    q_hbm, kv_hbm, off_hbm, w_ref, out_ref,
+    q_ref, kv_ref, off_ref, in_s,
+    qs, kvb, st, mx, acc, w2, att, attp, ysb, rlb, yrb, outb, xq, xp, xr,
+    up_s, peer_s, kv_r, wl_s, ws_s, wr_s, wf_s, wf_r, ax_s, ax_r, rl_s, rl_r, yd_s, yd_r, ys_s, ys_r, out_s, go, xq_s, xq_r, xr_s, xr_r,
 ):
     nhalf = nc // 2
     nz = nhalf // 2
     ny = nh // 2
-    half_rows = rows // 2
-    mrows = 2 * half_rows
+    part = rows // NR
+    mrows = QH * part
     width = QH * HD
     wrows = width // 2
+    hw = width // 2
 
     c = lax.axis_index("ctx")
     hd = lax.axis_index("head")
@@ -99,24 +102,24 @@
     def _():
         greet({"ctx": jnp.int32(extra)})
 
-    @pl.when(c == extra)
-    def _():
-        def body(d, carry):
-            greet({"ctx": d})
-            return carry
-        lax.fori_loop(0, nhalf, body, 0)
-
     def own_weights(j):
         col = pl.multiple_of((((y + j) % ny) * 2 + x) * width, 128)
         return pltpu.make_async_copy(
             w_ref.at[:, pl.ds(col, width)], w2.at[j, pl.ds(0, width), :], wl_s.at[j])
 
+    offsets_in = pltpu.make_async_copy(off_hbm, off_ref, in_s.at[0])
+    keys_in = pltpu.make_async_copy(kv_hbm, kv_ref, in_s.at[1])
+    queries_in = pltpu.make_async_copy(q_hbm, q_ref, in_s.at[2])
+    offsets_in.start()
+    keys_in.start()
+    queries_in.start()
     for j in range(ny):
         own_weights(j).start()
 
     lane = lax.broadcasted_iota(jnp.int32, (rows, HD), 1)
     token = lax.broadcasted_iota(jnp.int32, (rows, HD), 0) + c * rows
     start = jnp.zeros((rows, HD), jnp.int32)
+    offsets_in.wait()
     for d in range(off_ref.shape[0]):
         o = off_ref[d]
         start = jnp.maximum(start, jnp.where(token >= o, o, 0))
@@ -133,15 +136,26 @@
         field = field.astype(F32)
         return field * cosine + pltpu.roll(field, HD // 2, 1) * sine
 
+    keys_in.wait()
     kvb[own, 1] = kv_ref[1]
     kvb[own, 0] = rotate(kv_ref[0]).astype(BF)
 
-    pl.semaphore_wait(
-        barrier,
-        4 + (ny - 1)
-        + jnp.where(zz < nz - 1, 1, 0) + jnp.where(zz > 0, 1, 0)
-        + jnp.where(c < nhalf, 1, 0) + jnp.where(c == extra, nhalf, 0),
-    )
+    @pl.when(c != extra)
+    def _():
+        pl.semaphore_wait(barrier, 4 + (ny - 1) + jnp.where(zz < nz - 1, 1, 0) + jnp.where(zz > 0, 1, 0))
+
+    @pl.when(c == extra + 1)
+    def _():
+        pl.semaphore_signal(go, inc=1, device_id=peer, device_id_type=MESH)
+
+    if nz > 1:
+        @pl.when(c == extra + 2)
+        def _():
+            pl.semaphore_signal(go, inc=1, device_id=down, device_id_type=MESH)
+
+    @pl.when(c == extra)
+    def _():
+        pl.semaphore_wait(go, 2 if nz > 1 else 1)
 
     def send_up(slot, i, step):
         return remote(kvb.at[slot, i], kvb.at[slot, i], up_s.at[step, i], kv_r.at[slot, i], up)
@@ -155,6 +169,10 @@
             send_up(own, i, 0).start()
     for i in (1, 0):
         send_peer(own, i, 0).start()
+
+    @pl.when(c == extra)
+    def _():
+        pl.semaphore_wait(barrier, 4 + (ny - 1) + nhalf + (1 if nz > 1 else 0))
 
     wrow = pl.multiple_of(core * wrows, 128)
     wback = pl.multiple_of((1 - core) * wrows, 128)
@@ -182,18 +200,19 @@
             pass_weights(j).start()
 
     scale = HD ** (-0.5) * LOG2E
+    queries_in.wait()
     for h in range(QH):
         rot = (rotate(q_ref[:, h * HD:(h + 1) * HD]) * scale).astype(BF)
-        for r in range(2):
-            at = (r * QH + h) * half_rows
-            qs[at:at + half_rows, :] = rot[r * half_rows:(r + 1) * half_rows]
+        for r in range(NR):
+            at = r * mrows + h * part
+            qs[at:at + part, :] = rot[r * part:(r + 1) * part]
 
     def send_xq(d):
         return remote(xq, xq, xq_s.at[d], xq_r, {"ctx": d})
 
     @pl.when(c == extra)
     def _():
-        heads = [qs[h * half_rows:h * half_rows + 1, :] for h in range(QH)]
+        heads = [qs[h * part:h * part + 1, :] for h in range(QH)]
         xq[...] = jnp.concatenate(heads + [jnp.zeros((16 - QH, HD), BF)], axis=0)
 
         def body(d, carry):
@@ -208,18 +227,13 @@
         return jnp.tile(v, (1, n))
 
     def starts_of(t):
-        r = t // (QH // 2)
-        part = st[r * half_rows:(r + 1) * half_rows, :]
-        return jnp.concatenate([part] * 2, axis=0)
+        return jnp.concatenate([st[t * part:(t + 1) * part, :]] * QH, axis=0)
 
     def tokens_of(t, n):
-        r = t // (QH // 2)
-        i = lax.broadcasted_iota(jnp.int32, (mrows, n), 0) % half_rows
-        return i + (c * rows + r * half_rows)
-
-    ntile = QH
-
-    for t in range(ntile):
+        i = lax.broadcasted_iota(jnp.int32, (mrows, n), 0) % part
+        return i + (c * rows + t * part)
+
+    for t in range(NR):
         at = slice(t * mrows, (t + 1) * mrows)
         s = dot_t(qs[at, :], kvb[own, 0])
         key = lax.broadcasted_iota(jnp.int32, (mrows, rows), 1) + c * rows
@@ -230,10 +244,10 @@
         mx[at, :] = m
         acc[at, :] = dot(p, with_ones(kvb[own, 1]))
 
-    def update(first, keys, values, masked):
+    def update(first, keys, values, masked, tiles=range(NR)):
         n = keys.shape[0]
         values = with_ones(values)
-        for t in range(ntile):
+        for t in tiles:
             at = slice(t * mrows, (t + 1) * mrows)
             s = dot_t(qs[at, :], keys)
             if masked:
@@ -249,8 +263,7 @@
     def send_xp():
         return remote(xp, xr.at[own], xr_s, xr_r.at[own], {"ctx": jnp.int32(extra)})
 
-    @pl.when(c < nhalf)
-    def _():
+    def shared_token():
         send_xq(0).wait_recv()
         s = dot_t(xq[...], kvb[own, 0])
         m = jnp.broadcast_to(jnp.max(s, axis=1, keepdims=True), (16, HD))
@@ -267,11 +280,24 @@
         update((c - 1) * rows, kvb[other, 0], kvb[other, 1], True)
 
     late = min(5, nz - 1)
+    asked = min(2, nz - 1)
+
+    def both(chip):
+        for i in (1, 0):
+            send_peer(2 * chip + 1 - core, i, 0).wait_recv()
+        keys = jnp.concatenate([kvb[2 * chip, 0], kvb[2 * chip + 1, 0]], axis=0)
+        values = jnp.concatenate([kvb[2 * chip, 1], kvb[2 * chip + 1, 1]], axis=0)
+
+        @pl.when(half == 0)
+        def _():
+            update(0, keys, values, False)
+
+        @pl.when(half == 1)
+        def _():
+            update((half * nhalf + 2 * chip) * rows, keys, values, True)
 
     def step(k, carry):
-        chip = zz - k
-        mine = 2 * chip + core
-        theirs = 2 * chip + 1 - core
+        mine = 2 * (zz - k) + core
         for i in (1, 0):
             send_up(mine, i, 0).wait_recv()
 
@@ -279,18 +305,14 @@
             def _():
                 send_up(mine, i, k).start()
             send_peer(mine, i, k).start()
-        for i in (1, 0):
-            send_peer(theirs, i, 0).wait_recv()
-        keys = jnp.concatenate([kvb[2 * chip, 0], kvb[2 * chip + 1, 0]], axis=0)
-        values = jnp.concatenate([kvb[2 * chip, 1], kvb[2 * chip + 1, 1]], axis=0)
-
-        @pl.when(half == 0)
-        def _():
-            update(0, keys, values, False)
-
-        @pl.when(half == 1)
-        def _():
-            update((half * nhalf + 2 * chip) * rows, keys, values, True)
+
+        @pl.when(k > 1)
+        def _():
+            both(zz - k + 1)
+
+        @pl.when((k == asked) & (c < nhalf))
+        def _():
+            shared_token()
 
         @pl.when(k == late)
         def _():
@@ -298,6 +320,10 @@
         return carry
 
     lax.fori_loop(1, zz + 1, step, 0)
+
+    @pl.when((zz < asked) & (c < nhalf))
+    def _():
+        shared_token()
 
     @pl.when(zz < late)
     def _():
@@ -310,9 +336,9 @@
             return carry
         lax.fori_loop(0, nhalf, arrived, 0)
         pad = [jnp.zeros((8 - QH, HD), F32)]
-        mo = jnp.concatenate([mx[h * half_rows:h * half_rows + 1, :] for h in range(QH)] + pad, axis=0)
+        mo = jnp.concatenate([mx[h * part:h * part + 1, :] for h in range(QH)] + pad, axis=0)
         ao = jnp.concatenate(
-            [acc[h * half_rows:h * half_rows + 1, :] for h in range(QH)]
+            [acc[h * part:h * part + 1, :] for h in range(QH)]
             + [jnp.zeros((8 - QH, 2 * HD), F32)], axis=0)
         m = mo
         for d in range(nhalf):
@@ -321,15 +347,32 @@
         for d in range(nhalf):
             total = total + xr[d, :, HD:] * wide(jnp.exp2(xr[d, :, 0:HD] - m), 2)
         for h in range(QH):
-            acc[h * half_rows:h * half_rows + 1, :] = total[h:h + 1, :]
+            acc[h * part:h * part + 1, :] = total[h:h + 1, :]
 
     def send_att(r):
         return remote(att.at[r], attp.at[r], ax_s.at[r], ax_r.at[r], across)
 
-    for r in range(2):
+    def last(slot, tiles):
+        @pl.when((zz > 0) & (half == 0))
+        def _():
+            update(0, kvb[slot, 0], kvb[slot, 1], False, tiles)
+
+        @pl.when((zz > 0) & (half == 1))
+        def _():
+            update((half * nhalf + slot) * rows, kvb[slot, 0], kvb[slot, 1], True, tiles)
+
+    last(core, range(NR))
+
+    @pl.when(zz > 0)
+    def _():
+        for i in (1, 0):
+            send_peer(1 - core, i, 0).wait_recv()
+
+    for r in range(NR):
+        last(1 - core, [r])
         for h in range(QH):
-            at = (r * QH + h) * half_rows
-            block = acc[at:at + half_rows, :]
+            at = r * mrows + h * part
+            block = acc[at:at + part, :]
             att[r, :, h * HD:(h + 1) * HD] = (block[:, 0:HD] / block[:, HD:]).astype(BF)
         send_att(r).start()
 
@@ -337,29 +380,66 @@
         own_weights(j).wait()
         passed_weights(j).wait_recv()
 
-    def send_y(r, j):
-        return remote(ysb.at[r, j], yrb.at[r, j], y_s.at[r, j], y_r.at[r, j], along_y(j))
-
-    order = sorted(range(1, ny), key=lambda j: -min(j, ny - j))
-    for r in range(2):
+    low, high = pl.ds(0, hw), pl.ds(hw, hw)
+    ahead, back = along_y(1), along_y(ny - 1)
+
+    def relay(r, way):
+        cols, to = ((low, ahead), (high, back))[way]
+        return remote(ysb.at[r, 2, :, cols], rlb.at[r, way], rl_s.at[r, way], rl_r.at[r, way], to)
+
+    def direct(r, way):
+        cols, to = ((high, ahead), (low, back))[way]
+        j = (1, 3)[way]
+        return remote(ysb.at[r, j, :, cols], yrb.at[r, way, :, cols], yd_s.at[r, way], yd_r.at[r, way], to)
+
+    def summed(r, way):
+        cols, to = ((low, ahead), (high, back))[way]
+        j = (1, 3)[way]
+        return remote(ysb.at[r, j, :, cols], yrb.at[r, way, :, cols], ys_s.at[r, way], ys_r.at[r, way], to)
+
+    def join(r):
+        for way in range(2):
+            relay(r, way).wait_recv()
+            j = (1, 3)[way]
+            at = slice(way * hw, (way + 1) * hw)
+            ysb[r, j, :, at] = (ysb[r, j, :, at].astype(F32) + rlb[r, way].astype(F32)).astype(BF)
+            summed(r, way).start()
+
+    def write(r):
+        return pltpu.make_async_copy(outb.at[r], out_ref.at[pl.ds(r * part, part), :], out_s.at[r])
+
+    def total(r):
+        result = ysb[r, 0].astype(F32)
+        for way in range(2):
+            direct(r, way).wait_recv()
+            summed(r, way).wait_recv()
+            result = result + yrb[r, way].astype(F32)
+        outb[r] = result.astype(BF)
+        write(r).start()
+
+    for r in range(NR):
         send_att(r).wait_recv()
-        for j in order + [0]:
-            part = dot(att[r], w2[j, 0:width, :]) + dot(attp[r], w2[j, width:, :])
-            ysb[r, j] = part.astype(BF)
-            if j:
-                send_y(r, j).start()
-
-    for r in range(2):
-        total = ysb[r, 0].astype(F32)
-        for j in order[::-1]:
-            send_y(r, j).wait_recv()
-            total = total + yrb[r, j].astype(F32)
-        out_ref[r * half_rows:(r + 1) * half_rows, :] = total.astype(BF)
-
-    for r in range(2):
+        for j in (2, 1, 3, 0):
+            value = dot(att[r], w2[j, 0:width, :]) + dot(attp[r], w2[j, width:, :])
+            ysb[r, j] = value.astype(BF)
+            if j == 2:
+                relay(r, 0).start()
+                relay(r, 1).start()
+            elif j:
+                direct(r, j // 2).start()
+        if r:
+            join(r - 1)
+    join(NR - 1)
+    for r in range(NR):
+        total(r)
+
+    for r in range(NR):
+        write(r).wait()
         send_att(r).wait_send()
-        for j in order:
-            send_y(r, j).wait_send()
+        for way in range(2):
+            relay(r, way).wait_send()
+            direct(r, way).wait_send()
+            summed(r, way).wait_send()
     for j in range(ny):
         send_weights(j).wait_send()
         pass_weights(j).wait_send()
@@ -391,36 +471,43 @@
     nhalf = nc // 2
     nz = nhalf // 2
     ny = nh // 2
-    half_rows = rows // 2
+    part = rows // NR
     dma = pltpu.SemaphoreType.DMA
-    vmem = pl.BlockSpec(memory_space=pltpu.VMEM)
     return pl.pallas_call(
         functools.partial(kernel, nc, nh, rows),
         out_shape=jax.ShapeDtypeStruct((rows, width), BF),
-        in_specs=[vmem, vmem, pl.BlockSpec(memory_space=pltpu.SMEM), pl.BlockSpec(memory_space=pl.ANY)],
-        out_specs=vmem,
+        in_specs=[pl.BlockSpec(memory_space=pl.ANY)] * 4,
+        out_specs=pl.BlockSpec(memory_space=pl.ANY),
         scratch_shapes=[
+            pltpu.VMEM(queries.shape, BF),
+            pltpu.VMEM(keys_values.shape, BF),
+            pltpu.SMEM(offsets.shape, jnp.int32),
+            dma((3,)),
             pltpu.VMEM((QH * rows, HD), BF),
             pltpu.VMEM((nhalf, 2, rows, HD), BF),
             pltpu.VMEM((rows, HD), jnp.int32),
             pltpu.VMEM((QH * rows, HD), F32),
             pltpu.VMEM((QH * rows, 2 * HD), F32),
             pltpu.VMEM((ny, 2 * width, width), BF),
-            pltpu.VMEM((2, half_rows, width), BF),
-            pltpu.VMEM((2, half_rows, width), BF),
-            pltpu.VMEM((2, ny, half_rows, width), BF),
-            pltpu.VMEM((2, ny, half_rows, width), BF),
+            pltpu.VMEM((NR, part, width), BF),
+            pltpu.VMEM((NR, part, width), BF),
+            pltpu.VMEM((NR, ny, part, width), BF),
+            pltpu.VMEM((NR, 2, part, width // 2), BF),
+            pltpu.VMEM((NR, 2, part, width), BF),
+            pltpu.VMEM((NR, part, width), BF),
             pltpu.VMEM((16, HD), BF),
             pltpu.VMEM((8, 3 * HD), F32),
             pltpu.VMEM((nhalf, 8, 3 * HD), F32),
             dma((nz, 2)), dma((nz, 2)), dma((nhalf, 2)),
             dma((ny,)), dma((ny,)), dma((ny,)), dma((ny,)), dma((ny,)),
-            dma((2,)), dma((2,)),
-            dma((2, ny)), dma((2, ny)),
+            dma((NR,)), dma((NR,)),
+            dma((NR, 2)), dma((NR, 2)), dma((NR, 2)),
+            dma((NR, 2)), dma((NR, 2)), dma((NR, 2)),
+            dma((NR,)), pltpu.SemaphoreType.REGULAR,
             dma((nhalf,)), dma, dma, dma((nhalf,)),
         ],
         compiler_params=pltpu.CompilerParams(
-            collective_id=0, has_side_effects=True, vmem_limit_bytes=40 * 1024 * 1024),
+            collective_id=0, has_side_effects=True, vmem_limit_bytes=60 * 1024 * 1024),
         cost_estimate=pl.CostEstimate(flops=4 * 10 ** 9, bytes_accessed=6 * 2 ** 20, transcendentals=4 * 2 ** 20),
     )(queries, keys_values, offsets, w_out)
 

time: 65.2 us -> 52.6 us (0.81)
  the two profiles are of different devices: /device:TPU:227 before, /device:TPU:480 now
where the time goes in v2:
time: 52.6 us; the launch traced here: 52.4 us
  Pallas kernels  50.7 us (96%)
  local copies, waits for them, and re-layouts  1.67 us (3%)
    pallas_call x1, Pallas kernels, shards(): pl.pallas_call(functools.partial(kernel, nc, nh, rows), out_shape=jax.Sha...  50.7 us
    unnamed x1, local copies, waits for them, and re-layouts  1.67 us

profile of v2, /device:TPU:480, one launch (start us, length us, event | category | flops | bytes accessed | tf_op | source)
XLA Modules:
  0.0 52.4 jit_solution(9184302762001297252)
XLA Ops:
  0.0 50.7 %shard_map.46 = bf16[256,512]{1,0:T(8,128)(2,1)} custom-call(bf16[256,512]{1,0:T(8,128)(2,1)} %q_hbm.1, bf16[2,256,128]{2,1,0:T(8,128)(2,1)} %kv_hbm.1, s32[8]{0:T(128)} %off_hbm.1, bf16[512,4096]{1,0:T(8,128)(2,1)} %w_ref.1), custom_call_target="tpu_custom_call" | custom-call | flops 4000000000 | bytes 6291456 | tf_op jit(solution)/shard_map/pallas_call | solution.py:476
  50.7 1.7 %copy.6 = bf16[256,512]{1,0:T(8,128)(2,1)} copy(bf16[256,512]{1,0:T(8,128)(2,1)} %shard_map.46) | data formatting | bytes 524288

commit v3 on v2

--- a/solution.py
+++ b/solution.py
@@ -10,7 +10,8 @@
 
 HD = 128
 QH = 4
-NR = 4
+NR = 2
+ORDER = (2, 1, 3, 0)
 ROPE_BASE = 500000.0
 STRETCH = 16.0
 ANCHOR_LENGTH = 8192.0
@@ -41,10 +42,10 @@
 
 def kernel(
     nc, nh, rows,
-    q_hbm, kv_hbm, off_hbm, w_ref, out_ref,
-    q_ref, kv_ref, off_ref, in_s,
-    qs, kvb, st, mx, acc, w2, att, attp, ysb, rlb, yrb, outb, xq, xp, xr,
-    up_s, peer_s, kv_r, wl_s, ws_s, wr_s, wf_s, wf_r, ax_s, ax_r, rl_s, rl_r, yd_s, yd_r, ys_s, ys_r, out_s, go, xq_s, xq_r, xr_s, xr_r,
+    q_hbm, kv_hbm, off_hbm, w_ref, own_ref, ahead_ref, back_ref,
+    q_ref, k_ref, off_ref, in_s,
+    qs, kvb, st, mx, acc, w2, att, attp, half_sum, ysb, rlb, pas, xq, xp, xr,
+    up_s, peer_s, kv_r, wl_s, ws_s, wr_s, wf_s, wf_r, ax_s, ax_r, rl_s, rl_r, yd_s, yd_r, ys_s, ys_r, out_s, go, f1_s, f1_r, f2_s, xq_s, xq_r, xr_s, xr_r,
 ):
     nhalf = nc // 2
     nz = nhalf // 2
@@ -74,11 +75,20 @@
     w_to = {"head": hd + 1 - 2 * x, "dp": jnp.where(same_dp, dp, 1 - dp)}
     w_from = {"head": hd + 1 - 2 * x, "dp": jnp.where(same_dp, 1 - dp, dp)}
     extra = nhalf
+    dist = nhalf - 1
+    token = jnp.where(c == extra, 1, 0) + jnp.where(c == dist, nhalf - 1, 0)
 
     def along_y(j):
         return {"head": ((y + j) % ny) * 2 + x}
 
     barrier = pltpu.get_barrier_semaphore()
+
+    wrap = nz == 8
+    up_steps = jnp.where(half == 1, nz - 2, nz - 1) if wrap else nz - 1
+    relay_at = 2 * (nz - 2)
+    source = (half == 1) & (zz == 0)
+    sink = (half == 1) & (zz == nz - 1)
+    far = jnp.where(source, 1, 0)
 
     def greet(device):
         pl.semaphore_signal(barrier, inc=1, device_id=device, device_id_type=MESH)
@@ -98,9 +108,25 @@
     def _():
         greet(down)
 
-    @pl.when(c < nhalf)
+    @pl.when(c < dist)
+    def _():
+        greet({"ctx": jnp.int32(dist)})
+
+    @pl.when(c == dist)
     def _():
         greet({"ctx": jnp.int32(extra)})
+
+    if wrap:
+        @pl.when(c == relay_at)
+        def _():
+            for column in range(2):
+                greet({"ctx": jnp.int32(nhalf + column)})
+
+        @pl.when(sink)
+        def _():
+            greet({"ctx": jnp.int32(relay_at)})
+
+    order = [j for j in ORDER if j < ny]
 
     def own_weights(j):
         col = pl.multiple_of((((y + j) % ny) * 2 + x) * width, 128)
@@ -108,13 +134,67 @@
             w_ref.at[:, pl.ds(col, width)], w2.at[j, pl.ds(0, width), :], wl_s.at[j])
 
     offsets_in = pltpu.make_async_copy(off_hbm, off_ref, in_s.at[0])
-    keys_in = pltpu.make_async_copy(kv_hbm, kv_ref, in_s.at[1])
+    keys_in = pltpu.make_async_copy(kv_hbm.at[0], k_ref, in_s.at[1])
+    values_in = pltpu.make_async_copy(kv_hbm.at[1], kvb.at[own, 1], in_s.at[3])
     queries_in = pltpu.make_async_copy(q_hbm, q_ref, in_s.at[2])
+    values_in.start()
     offsets_in.start()
     keys_in.start()
     queries_in.start()
     for j in range(ny):
         own_weights(j).start()
+
+    near = 4 + (ny - 1) + token + jnp.where(zz < nz - 1, 1, 0) + jnp.where(zz > 0, 1, 0)
+    if wrap:
+        @pl.when(c != relay_at)
+        def _():
+            pl.semaphore_wait(barrier, near + far)
+
+        @pl.when(c == relay_at + 1)
+        def _():
+            pl.semaphore_signal(go, inc=1, device_id=peer, device_id_type=MESH)
+
+        @pl.when(c == relay_at + 2)
+        def _():
+            pl.semaphore_signal(go, inc=1, device_id=down, device_id_type=MESH)
+
+        @pl.when(c == relay_at)
+        def _():
+            pl.semaphore_wait(go, 2)
+    else:
+        pl.semaphore_wait(barrier, near)
+
+    def send_up(slot, i, step):
+        return remote(kvb.at[slot, i], kvb.at[slot, i], up_s.at[step, i], kv_r.at[slot, i], up)
+
+    def send_peer(slot, i, step):
+        return remote(kvb.at[slot, i], kvb.at[slot, i], peer_s.at[step, i], kv_r.at[slot, i], peer)
+
+    def send_own(i):
+        @pl.when(zz < nz - 1)
+        def _():
+            send_up(own, i, 0).start()
+
+        if wrap:
+            for column in range(2):
+                @pl.when(source & (core == column))
+                def _():
+                    first_leg(i, column).start()
+
+        @pl.when(core == 0)
+        def _():
+            send_peer(own, i, 0).start()
+
+    def first_leg(i, column):
+        return remote(kvb.at[own, i], pas.at[column, i], f1_s.at[i], f1_r.at[column, i], {"ctx": jnp.int32(relay_at)})
+
+    def second_leg(i, column):
+        return remote(
+            pas.at[column, i], kvb.at[column, i], f2_s.at[column, i], kv_r.at[column, i],
+            {"ctx": jnp.int32(nhalf + 2 * (nz - 1) + column)})
+
+    values_in.wait()
+    send_own(1)
 
     lane = lax.broadcasted_iota(jnp.int32, (rows, HD), 1)
     token = lax.broadcasted_iota(jnp.int32, (rows, HD), 0) + c * rows
@@ -137,42 +217,13 @@
         return field * cosine + pltpu.roll(field, HD // 2, 1) * sine
 
     keys_in.wait()
-    kvb[own, 1] = kv_ref[1]
-    kvb[own, 0] = rotate(kv_ref[0]).astype(BF)
-
-    @pl.when(c != extra)
-    def _():
-        pl.semaphore_wait(barrier, 4 + (ny - 1) + jnp.where(zz < nz - 1, 1, 0) + jnp.where(zz > 0, 1, 0))
-
-    @pl.when(c == extra + 1)
-    def _():
-        pl.semaphore_signal(go, inc=1, device_id=peer, device_id_type=MESH)
-
-    if nz > 1:
-        @pl.when(c == extra + 2)
-        def _():
-            pl.semaphore_signal(go, inc=1, device_id=down, device_id_type=MESH)
-
-    @pl.when(c == extra)
-    def _():
-        pl.semaphore_wait(go, 2 if nz > 1 else 1)
-
-    def send_up(slot, i, step):
-        return remote(kvb.at[slot, i], kvb.at[slot, i], up_s.at[step, i], kv_r.at[slot, i], up)
-
-    def send_peer(slot, i, step):
-        return remote(kvb.at[slot, i], kvb.at[slot, i], peer_s.at[step, i], kv_r.at[slot, i], peer)
-
-    @pl.when(zz < nz - 1)
-    def _():
-        for i in (1, 0):
-            send_up(own, i, 0).start()
-    for i in (1, 0):
-        send_peer(own, i, 0).start()
-
-    @pl.when(c == extra)
-    def _():
-        pl.semaphore_wait(barrier, 4 + (ny - 1) + nhalf + (1 if nz > 1 else 0))
+    kvb[own, 0] = rotate(k_ref[...]).astype(BF)
+    send_own(0)
+
+    if wrap:
+        @pl.when(c == relay_at)
+        def _():
+            pl.semaphore_wait(barrier, near + 2)
 
     wrow = pl.multiple_of(core * wrows, 128)
     wback = pl.multiple_of((1 - core) * wrows, 128)
@@ -191,13 +242,12 @@
         at = w2.at[j, pl.ds(width + wback, wrows), :]
         return remote(at, at, wf_s.at[j], wf_r.at[j], peer)
 
-    for j in range(ny):
+    for j in order:
         send_weights(j).start()
 
-    def forward_weights():
-        for j in range(ny):
-            send_weights(j).wait_recv()
-            pass_weights(j).start()
+    def forward_weights(j):
+        send_weights(j).wait_recv()
+        pass_weights(j).start()
 
     scale = HD ** (-0.5) * LOG2E
     queries_in.wait()
@@ -207,18 +257,26 @@
             at = r * mrows + h * part
             qs[at:at + part, :] = rot[r * part:(r + 1) * part]
 
-    def send_xq(d):
+    def hand_over():
+        return remote(xq, xq, xq_s.at[0], xq_r, {"ctx": jnp.int32(dist)})
+
+    def hand_out(d):
         return remote(xq, xq, xq_s.at[d], xq_r, {"ctx": d})
 
     @pl.when(c == extra)
     def _():
         heads = [qs[h * part:h * part + 1, :] for h in range(QH)]
         xq[...] = jnp.concatenate(heads + [jnp.zeros((16 - QH, HD), BF)], axis=0)
+        hand_over().start()
+
+    @pl.when(c == dist)
+    def _():
+        hand_out(0).wait_recv()
 
         def body(d, carry):
-            send_xq(d).start()
+            hand_out(d).start()
             return carry
-        lax.fori_loop(0, nhalf, body, 0)
+        lax.fori_loop(0, nhalf - 1, body, 0)
 
     def with_ones(v):
         return jnp.concatenate([v, jnp.ones(v.shape, BF)], axis=1)
@@ -263,24 +321,26 @@
     def send_xp():
         return remote(xp, xr.at[own], xr_s, xr_r.at[own], {"ctx": jnp.int32(extra)})
 
-    def shared_token():
-        send_xq(0).wait_recv()
+    def answer_token():
+        @pl.when(c != dist)
+        def _():
+            hand_over().wait_recv()
+
         s = dot_t(xq[...], kvb[own, 0])
         m = jnp.broadcast_to(jnp.max(s, axis=1, keepdims=True), (16, HD))
         p = jnp.exp2(s - wide(m, rows // HD)).astype(BF)
-        xp[:, 0:HD] = m[0:8]
-        xp[:, HD:] = dot(p, with_ones(kvb[own, 1]))[0:8]
+        sums = dot(p, with_ones(kvb[own, 1]))
+        xp[0:QH, :] = sums[0:QH, 0:HD]
+        xp[QH:2 * QH, :] = jnp.where(lane[0:QH] < HD // 2, m[0:QH], sums[0:QH, HD:])
         send_xp().start()
 
-    for i in (1, 0):
-        send_peer(other, i, 0).wait_recv()
-
     @pl.when(core == 1)
     def _():
+        for i in (1, 0):
+            send_peer(other, i, 0).wait_recv()
         update((c - 1) * rows, kvb[other, 0], kvb[other, 1], True)
 
-    late = min(5, nz - 1)
-    asked = min(2, nz - 1)
+    steps = jnp.minimum(zz, up_steps)
 
     def both(chip):
         for i in (1, 0):
@@ -301,7 +361,7 @@
         for i in (1, 0):
             send_up(mine, i, 0).wait_recv()
 
-            @pl.when(zz < nz - 1)
+            @pl.when((zz < nz - 1) & (k < up_steps))
             def _():
                 send_up(mine, i, k).start()
             send_peer(mine, i, k).start()
@@ -310,24 +370,45 @@
         def _():
             both(zz - k + 1)
 
-        @pl.when((k == asked) & (c < nhalf))
-        def _():
-            shared_token()
-
-        @pl.when(k == late)
-        def _():
-            forward_weights()
+        @pl.when((k == 3) & (zz > 3) & (c < nhalf))
+        def _():
+            answer_token()
+
+        for i, j in enumerate(order):
+            @pl.when(k == i + 2)
+            def _():
+                forward_weights(j)
+
+        if wrap:
+            @pl.when(sink & (k == nz - 3))
+            def _():
+                for i in (1, 0):
+                    send_peer(core, i, 0).wait_recv()
+                    send_peer(core, i, nz - 1).start()
+
+            @pl.when((c == relay_at) & (k == 2))
+            def _():
+                for column in range(2):
+                    for i in (1, 0):
+                        first_leg(i, column).wait_recv()
+                        second_leg(i, column).start()
         return carry
 
-    lax.fori_loop(1, zz + 1, step, 0)
-
-    @pl.when((zz < asked) & (c < nhalf))
-    def _():
-        shared_token()
-
-    @pl.when(zz < late)
-    def _():
-        forward_weights()
+    lax.fori_loop(1, steps + 1, step, 0)
+
+    @pl.when((zz <= 3) & (c < nhalf))
+    def _():
+        answer_token()
+
+    for i, j in enumerate(order):
+        @pl.when(steps < i + 2)
+        def _():
+            forward_weights(j)
+
+    if wrap:
+        @pl.when(sink)
+        def _():
+            both(zz - up_steps)
 
     @pl.when(c == extra)
     def _():
@@ -335,17 +416,14 @@
             remote(xp, xr.at[d], xr_s, xr_r.at[d], {"ctx": jnp.int32(0)}).wait_recv()
             return carry
         lax.fori_loop(0, nhalf, arrived, 0)
-        pad = [jnp.zeros((8 - QH, HD), F32)]
-        mo = jnp.concatenate([mx[h * part:h * part + 1, :] for h in range(QH)] + pad, axis=0)
-        ao = jnp.concatenate(
-            [acc[h * part:h * part + 1, :] for h in range(QH)]
-            + [jnp.zeros((8 - QH, 2 * HD), F32)], axis=0)
-        m = mo
-        for d in range(nhalf):
-            m = jnp.maximum(m, xr[d, :, 0:HD])
+        mo = jnp.concatenate([mx[h * part:h * part + 1, :] for h in range(QH)], axis=0)
+        ao = jnp.concatenate([acc[h * part:h * part + 1, :] for h in range(QH)], axis=0)
+        tops = [jnp.broadcast_to(xr[d, QH:2 * QH, 0:1], (QH, HD)) for d in range(nhalf)]
+        m = functools.reduce(jnp.maximum, tops, mo)
         total = ao * wide(jnp.exp2(mo - m), 2)
         for d in range(nhalf):
-            total = total + xr[d, :, HD:] * wide(jnp.exp2(xr[d, :, 0:HD] - m), 2)
+            weight = jnp.broadcast_to(xr[d, QH:2 * QH, HD // 2:HD // 2 + 1], (QH, HD))
+            total = total + jnp.concatenate([xr[d, 0:QH, :], weight], axis=1) * wide(jnp.exp2(tops[d] - m), 2)
         for h in range(QH):
             acc[h * part:h * part + 1, :] = total[h:h + 1, :]
 
@@ -376,8 +454,10 @@
             att[r, :, h * HD:(h + 1) * HD] = (block[:, 0:HD] / block[:, HD:]).astype(BF)
         send_att(r).start()
 
-    for j in range(ny):
+    for j in order:
         own_weights(j).wait()
+        half_sum[j] = dot(att[...].reshape(rows, width), w2[j, 0:width, :])
+    for j in order:
         passed_weights(j).wait_recv()
 
     low, high = pl.ds(0, hw), pl.ds(hw, hw)
@@ -387,15 +467,18 @@
         cols, to = ((low, ahead), (high, back))[way]
         return remote(ysb.at[r, 2, :, cols], rlb.at[r, way], rl_s.at[r, way], rl_r.at[r, way], to)
 
+    def landing(r, way, cols):
+        return (ahead_ref, back_ref)[way].at[pl.ds(r * part, part), cols]
+
     def direct(r, way):
         cols, to = ((high, ahead), (low, back))[way]
         j = (1, 3)[way]
-        return remote(ysb.at[r, j, :, cols], yrb.at[r, way, :, cols], yd_s.at[r, way], yd_r.at[r, way], to)
+        return remote(ysb.at[r, j, :, cols], landing(r, way, cols), yd_s.at[r, way], yd_r.at[r, way], to)
 
     def summed(r, way):
         cols, to = ((low, ahead), (high, back))[way]
         j = (1, 3)[way]
-        return remote(ysb.at[r, j, :, cols], yrb.at[r, way, :, cols], ys_s.at[r, way], ys_r.at[r, way], to)
+        return remote(ysb.at[r, j, :, cols], landing(r, way, cols), ys_s.at[r, way], ys_r.at[r, way], to)
 
     def join(r):
         for way in range(2):
@@ -406,32 +489,27 @@
             summed(r, way).start()
 
     def write(r):
-        return pltpu.make_async_copy(outb.at[r], out_ref.at[pl.ds(r * part, part), :], out_s.at[r])
-
-    def total(r):
-        result = ysb[r, 0].astype(F32)
-        for way in range(2):
-            direct(r, way).wait_recv()
-            summed(r, way).wait_recv()
-            result = result + yrb[r, way].astype(F32)
-        outb[r] = result.astype(BF)
-        write(r).start()
+        return pltpu.make_async_copy(ysb.at[r, 0], own_ref.at[pl.ds(r * part, part), :], out_s.at[r])
 
     for r in range(NR):
         send_att(r).wait_recv()
-        for j in (2, 1, 3, 0):
-            value = dot(att[r], w2[j, 0:width, :]) + dot(attp[r], w2[j, width:, :])
+        for j in ORDER:
+            value = half_sum[j, r * part:(r + 1) * part, :] + dot(attp[r], w2[j, width:, :])
             ysb[r, j] = value.astype(BF)
             if j == 2:
                 relay(r, 0).start()
                 relay(r, 1).start()
             elif j:
                 direct(r, j // 2).start()
+            else:
+                write(r).start()
         if r:
             join(r - 1)
     join(NR - 1)
     for r in range(NR):
-        total(r)
+        for way in range(2):
+            direct(r, way).wait_recv()
+            summed(r, way).wait_recv()
 
     for r in range(NR):
         write(r).wait()
@@ -446,23 +524,41 @@
 
     def sent(k, carry):
         for i in (1, 0):
-            @pl.when(zz < nz - 1)
+            @pl.when((zz < nz - 1) & (k < up_steps))
             def _():
                 send_up(own, i, k).wait_send()
-            send_peer(own, i, k).wait_send()
+
+            @pl.when((k > 0) | (core == 0))
+            def _():
+                send_peer(own, i, k).wait_send()
         return carry
     lax.fori_loop(0, zz + 1, sent, 0)
 
+    if wrap:
+        for i in (1, 0):
+            @pl.when(source)
+            def _():
+                first_leg(i, 0).wait_send()
+
+            @pl.when(c == relay_at)
+            def _():
+                for column in range(2):
+                    second_leg(i, column).wait_send()
+
     @pl.when(c < nhalf)
     def _():
         send_xp().wait_send()
 
     @pl.when(c == extra)
     def _():
+        hand_over().wait_send()
+
+    @pl.when(c == dist)
+    def _():
         def body(d, carry):
-            send_xq(d).wait_send()
+            hand_out(d).wait_send()
             return carry
-        lax.fori_loop(0, nhalf, body, 0)
+        lax.fori_loop(0, nhalf - 1, body, 0)
 
 
 def shards(nc, nh, queries, keys_values, offsets, w_out):
@@ -473,16 +569,16 @@
     ny = nh // 2
     part = rows // NR
     dma = pltpu.SemaphoreType.DMA
-    return pl.pallas_call(
+    parts = pl.pallas_call(
         functools.partial(kernel, nc, nh, rows),
-        out_shape=jax.ShapeDtypeStruct((rows, width), BF),
+        out_shape=[jax.ShapeDtypeStruct((rows, width), BF)] * 3,
         in_specs=[pl.BlockSpec(memory_space=pl.ANY)] * 4,
-        out_specs=pl.BlockSpec(memory_space=pl.ANY),
+        out_specs=[pl.BlockSpec(memory_space=pl.ANY)] * 3,
         scratch_shapes=[
             pltpu.VMEM(queries.shape, BF),
-            pltpu.VMEM(keys_values.shape, BF),
+            pltpu.VMEM((rows, HD), BF),
             pltpu.SMEM(offsets.shape, jnp.int32),
-            dma((3,)),
+            dma((4,)),
             pltpu.VMEM((QH * rows, HD), BF),
             pltpu.VMEM((nhalf, 2, rows, HD), BF),
             pltpu.VMEM((rows, HD), jnp.int32),
@@ -491,25 +587,27 @@
             pltpu.VMEM((ny, 2 * width, width), BF),
             pltpu.VMEM((NR, part, width), BF),
             pltpu.VMEM((NR, part, width), BF),
+            pltpu.VMEM((ny, rows, width), F32),
             pltpu.VMEM((NR, ny, part, width), BF),
             pltpu.VMEM((NR, 2, part, width // 2), BF),
-            pltpu.VMEM((NR, 2, part, width), BF),
-            pltpu.VMEM((NR, part, width), BF),
+            pltpu.VMEM((2, 2, rows, HD), BF),
             pltpu.VMEM((16, HD), BF),
-            pltpu.VMEM((8, 3 * HD), F32),
-            pltpu.VMEM((nhalf, 8, 3 * HD), F32),
+            pltpu.VMEM((2 * QH, HD), F32),
+            pltpu.VMEM((nhalf, 2 * QH, HD), F32),
             dma((nz, 2)), dma((nz, 2)), dma((nhalf, 2)),
             dma((ny,)), dma((ny,)), dma((ny,)), dma((ny,)), dma((ny,)),
             dma((NR,)), dma((NR,)),
             dma((NR, 2)), dma((NR, 2)), dma((NR, 2)),
             dma((NR, 2)), dma((NR, 2)), dma((NR, 2)),
             dma((NR,)), pltpu.SemaphoreType.REGULAR,
+            dma((2,)), dma((2, 2)), dma((2, 2)),
             dma((nhalf,)), dma, dma, dma((nhalf,)),
         ],
         compiler_params=pltpu.CompilerParams(
             collective_id=0, has_side_effects=True, vmem_limit_bytes=60 * 1024 * 1024),
         cost_estimate=pl.CostEstimate(flops=4 * 10 ** 9, bytes_accessed=6 * 2 ** 20, transcendentals=4 * 2 ** 20),
     )(queries, keys_values, offsets, w_out)
+    return (parts[0].astype(F32) + parts[1].astype(F32) + parts[2].astype(F32)).astype(BF)
 
 
 def solution(mesh):

time: 52.6 us -> 51 us (0.970)
  Pallas kernels: 50.7 us -> 48.4 us
  other arithmetic: 0 us -> 1.91 us
  local copies, waits for them, and re-layouts: 1.67 us -> 0 us
    pallas_call x1, Pallas kernels: 50.7 us -> 48.4 us  [shards(): pl.pallas_call(functools.partial(kernel, nc, nh, rows), out_shape=[jax.Sh...]
    convert_element_type x0 -> x1, other arithmetic: none -> 1.91 us  [shards(): (parts[0].astype(F32) + parts[1].astype(F32) + parts[2].astype(F32)).asty...]
    unnamed x1 -> x0, local copies, waits for them, and re-layouts: 1.67 us -> none
where the time goes in v3:
time: 51 us; the launch traced here: 50.3 us
  Pallas kernels  48.4 us (95%)
  other arithmetic  1.91 us (4%)
    pallas_call x1, Pallas kernels, shards(): pl.pallas_call(functools.partial(kernel, nc, nh, rows), out_shape=[jax.Sh...  48.4 us
    convert_element_type x1, other arithmetic, shards(): (parts[0].astype(F32) + parts[1].astype(F32) + parts[2].astype(F32)).asty...  1.91 us

profile of v3, /device:TPU:480, one launch (start us, length us, event | category | flops | bytes accessed | tf_op | source)
XLA Modules:
  0.0 50.3 jit_solution(7597535301860107751)
XLA Ops:
  0.0 48.4 %shard_map.46 = (bf16[256,512]{1,0:T(8,128)(2,1)}, bf16[256,512]{1,0:T(8,128)(2,1)}, bf16[256,512]{1,0:T(8,128)(2,1)}) custom-call(bf16[256,512]{1,0:T(8,128)(2,1)} %q_hbm.1, bf16[2,256,128]{2,1,0:T(8,128)(2,1)} %kv_hbm.1, s32[8]{0:T(128)} %off_hbm.1, bf16[512,4096]{1,0:T(8,128)(2,1)} %w_ref.1), custom_call_target="tpu_custom_call" | custom-call | flops 4000000000 | bytes 6291456 | tf_op jit(solution)/shard_map/pallas_call | solution.py:572
  48.4 1.9 %add_convert_fusion = bf16[256,512]{1,0:T(8,128)(2,1)} fusion(bf16[256,512]{1,0:T(8,128)(2,1)} %get-tuple-element.10, bf16[256,512]{1,0:T(8,128)(2,1)} %get-tuple-element.9, bf16[256,512]{1,0:T(8,128)(2,1)} %get-tuple-element.8), kind=kLoop, calls=%fused_computation | loop fusion | flops 786432 | bytes 1048576 | tf_op jit(solution)/shard_map/convert_element_type | solution.py:610

commit v4 on v3

--- a/solution.py
+++ b/solution.py
@@ -386,6 +386,10 @@
                     send_peer(core, i, 0).wait_recv()
                     send_peer(core, i, nz - 1).start()
 
+            @pl.when(sink & (k == nz - 2))
+            def _():
+                both(0)
+
             @pl.when((c == relay_at) & (k == 2))
             def _():
                 for column in range(2):
@@ -404,11 +408,6 @@
         @pl.when(steps < i + 2)
         def _():
             forward_weights(j)
-
-    if wrap:
-        @pl.when(sink)
-        def _():
-            both(zz - up_steps)
 
     @pl.when(c == extra)
     def _():
@@ -439,15 +438,16 @@
         def _():
             update((half * nhalf + slot) * rows, kvb[slot, 0], kvb[slot, 1], True, tiles)
 
-    last(core, range(NR))
+    bottom = 2 * (zz - steps)
+    last(bottom + core, range(NR))
 
     @pl.when(zz > 0)
     def _():
         for i in (1, 0):
-            send_peer(1 - core, i, 0).wait_recv()
+            send_peer(bottom + 1 - core, i, 0).wait_recv()
 
     for r in range(NR):
-        last(1 - core, [r])
+        last(bottom + 1 - core, [r])
         for h in range(QH):
             at = r * mrows + h * part
             block = acc[at:at + part, :]

time: 51 us -> 50 us (0.980)
    pallas_call x1, Pallas kernels: 48.4 us -> 47.9 us  [shards(): pl.pallas_call(functools.partial(kernel, nc, nh, rows), out_shape=[jax.Sh...]
where the time goes in v4:
time: 50 us; the launch traced here: 49.8 us
  Pallas kernels  47.9 us (96%)
  other arithmetic  1.91 us (4%)
    pallas_call x1, Pallas kernels, shards(): pl.pallas_call(functools.partial(kernel, nc, nh, rows), out_shape=[jax.Sh...  47.9 us
    convert_element_type x1, other arithmetic, shards(): (parts[0].astype(F32) + parts[1].astype(F32) + parts[2].astype(F32)).asty...  1.91 us

profile of v4, /device:TPU:480, one launch (start us, length us, event | category | flops | bytes accessed | tf_op | source)
XLA Modules:
  0.0 49.8 jit_solution(11297115485298546743)
XLA Ops:
  0.0 47.9 %shard_map.46 = (bf16[256,512]{1,0:T(8,128)(2,1)}, bf16[256,512]{1,0:T(8,128)(2,1)}, bf16[256,512]{1,0:T(8,128)(2,1)}) custom-call(bf16[256,512]{1,0:T(8,128)(2,1)} %q_hbm.1, bf16[2,256,128]{2,1,0:T(8,128)(2,1)} %kv_hbm.1, s32[8]{0:T(128)} %off_hbm.1, bf16[512,4096]{1,0:T(8,128)(2,1)} %w_ref.1), custom_call_target="tpu_custom_call" | custom-call | flops 4000000000 | bytes 6291456 | tf_op jit(solution)/shard_map/pallas_call | solution.py:572
  47.9 1.9 %add_convert_fusion = bf16[256,512]{1,0:T(8,128)(2,1)} fusion(bf16[256,512]{1,0:T(8,128)(2,1)} %get-tuple-element.10, bf16[256,512]{1,0:T(8,128)(2,1)} %get-tuple-element.9, bf16[256,512]{1,0:T(8,128)(2,1)} %get-tuple-element.8), kind=kLoop, calls=%fused_computation | loop fusion | flops 786432 | bytes 1048576 | tf_op jit(solution)/shard_map/convert_element_type | solution.py:610
